TPU v7x, 512 devices: a whole 4x4x16 slice. The times are simulated.
512 devices in a mesh: row: 32 (over x, y, core), col: 16 (over z).
Axes of the slice: x: 4, y: 4, z: 16, core: 2. Of those that a mesh axis runs over, the one named last changes fastest.
Arguments:
- blocks: float32 [32, 192, 256, 256], P('row', 'col'), may hold values from -0.078125 to 0.078125
- block_rows: int32 [32, 192], P('row', 'col'), may hold values from 0 to 3, as said below
- block_cols: int32 [32, 192], P('row', 'col'), may hold values from 0 to 7
- live_count: int32 [32, 16], P('row', 'col'), may hold values from 1 to 12
- primal_now: float32 [16, 2048, 128], P('col', 'row'), may hold values from -3 to 3
- primal_prev: float32 [16, 2048, 128], P('col', 'row'), may hold values from -3 to 3
- dual_now: float32 [32, 1024, 128], P('row', 'col'), may hold values from 0 to 1
- row_bound: float32 [32, 1024, 128], P('row', 'col'), may hold values from -6 to 6
- objective: float32 [16, 2048, 128], P('col', 'row'), may hold values from -6 to 6
- lower_bound: float32 [16, 2048, 128], P('col', 'row'), may hold values from -1 to -0.2
- upper_bound: float32 [16, 2048, 128], P('col', 'row'), may hold values from 0.2 to 1
Outputs:
- primal_out: float32 [16, 2048, 128], P('col', 'row')
- dual_out: float32 [32, 1024, 128], P('row', 'col')
Inputs may be any that keep to these rules, and one draw needn't show every extreme that they name: On each device the 12 pairs (block_rows, block_cols) are distinct.
All inputs are finite; a program needn't handle non-finite values.
Results may differ from a plain program's by a relative error of at most 0.0001.
Values sent between devices are 32-bit elements; how exact they have to be, the bound alone decides.
A program may use at most 64 MiB of HBM per device.

v0:
```python
import jax
import jax.numpy as jnp
from jax import lax
from jax.sharding import PartitionSpec as P

RB_DEV = 4
CB_DEV = 8
ITERS = 2


dual_step = 0.3
primal_step = 0.3


def on_device(
    blocks,
    block_rows,
    block_cols,
    live_count,
    primal_now,
    primal_prev,
    dual_now,
    row_bound,
    objective,
    lower_bound,
    upper_bound,
):
    highest = lax.Precision.HIGHEST
    tiles = blocks[0]
    tile_size = tiles.shape[1]
    scenarios = primal_now.shape[2]
    filled = live_count[0, 0]
    rows_list = block_rows[0]
    cols_list = block_cols[0]
    in_use = (jnp.arange(tiles.shape[0], dtype=jnp.int32) < filled).astype(jnp.float32)
    row_pick = jax.nn.one_hot(rows_list, RB_DEV, dtype=jnp.float32)
    col_pick = jax.nn.one_hot(cols_list, CB_DEV, dtype=jnp.float32)
    row_live = row_pick * in_use[:, None]
    col_live = col_pick * in_use[:, None]
    current = primal_now[0]
    previous = primal_prev[0]
    dual_vec = dual_now[0]
    for step in range(ITERS):
        extrapolated = 2.0 * current - previous
        whole_cols = lax.all_gather(extrapolated, "row", axis=0, tiled=True)
        forward_spread = whole_cols.reshape(CB_DEV, tile_size, scenarios)
        forward_picked = jnp.einsum("sc,cjb->sjb", col_live, forward_spread, precision=highest)
        forward_product = jnp.einsum("sij,sjb->sib", tiles, forward_picked, precision=highest)
        image = lax.psum_scatter(
            jnp.einsum("sr,sib->rib", row_pick, forward_product, precision=highest).reshape(
                RB_DEV * tile_size, scenarios
            ),
            "col",
            scatter_dimension=0,
            tiled=True,
        )
        dual_vec = jnp.maximum(dual_vec + dual_step * (row_bound[0] - image), 0.0)
        whole_rows = lax.all_gather(dual_vec, "col", axis=0, tiled=True)
        spread = whole_rows.reshape(RB_DEV, tile_size, scenarios)
        picked = jnp.einsum("sr,rib->sib", row_live, spread, precision=highest)
        product = jnp.einsum("sij,sib->sjb", tiles, picked, precision=highest)
        adjoint = lax.psum_scatter(
            jnp.einsum("sc,sjb->cjb", col_pick, product, precision=highest).reshape(
                CB_DEV * tile_size, scenarios
            ),
            "row",
            scatter_dimension=0,
            tiled=True,
        )
        previous = current
        current = jnp.minimum(
            jnp.maximum(current - primal_step * (objective[0] - adjoint), lower_bound[0]),
            upper_bound[0],
        )
    return (current[None], dual_vec[None])


def solution(mesh):
    in_specs = (
        P("row", "col", None, None),
        P("row", "col"),
        P("row", "col"),
        P("row", "col"),
        P("col", "row", None),
        P("col", "row", None),
        P("row", "col", None),
        P("row", "col", None),
        P("col", "row", None),
        P("col", "row", None),
        P("col", "row", None),
    )
    out_specs = (P("col", "row", None), P("row", "col", None))
    return jax.shard_map(
        on_device, mesh=mesh, in_specs=in_specs, out_specs=out_specs, check_vma=False
    )
```

profile of v0, /device:TPU:1, one launch (start us, length us, event | category | flops | bytes accessed | tf_op | source)
XLA Modules:
  0.0 597.8 jit_solution(15678235338718240190)
XLA Ops:
  7.2 1.5 bitcast_subtract_fusion
  9.5 66.1 %all-gather.3.cloned.1.call-done = f32[2048,128]{1,0:T(8,128)} async-done(((f32[64,128]{1,0:T(8,128)}), f32[2048,128]{1,0:T(8,128)}) %all-gather.3.cloned.1.call-update) | async-done | bytes 1048592 | tf_op jit(solution)/shard_map/all_gather | solution.py:45
  75.6 3.4 fusion.22
  79.0 4.9 fusion.6
  83.9 3.0 copy.19
  86.9 2.4 fusion.14
  89.3 0.8 copy.13
  90.2 57.3 %reduce-scatter.5.cloned.1.call-done = f32[64,128]{1,0:T(8,128)} async-done(((f32[1024,128]{1,0:T(8,128)}), f32[64,128]{1,0:T(8,128)}) %reduce-scatter.5.cloned.1.call-update) | async-done | bytes 32784 | tf_op jit(solution)/shard_map/reduce_scatter | solution.py:49
  147.5 0.8 fusion.31
  148.2 23.7 %all_gather.13 = f32[1024,128]{1,0:T(8,128)S(1)} all-gather(f32[64,128]{1,0:T(8,128)S(1)} %fusion.31), channel_id=1, replica_groups=mesh['row'=32,'col'=16] {'col'}, dimensions={0}, use_global_device_ids=true | all-gather | bytes 557056 | tf_op jit(solution)/shard_map/all_gather | solution.py:58
  171.9 2.1 fusion.26
  174.0 4.5 fusion.4
  178.5 3.0 copy.22
  181.4 2.4 fusion.12
  183.9 1.2 copy.14
  185.1 115.9 %reduce-scatter.7.cloned.1.call-done = f32[64,128]{1,0:T(8,128)} async-done(((f32[2048,128]{1,0:T(8,128)}), f32[64,128]{1,0:T(8,128)}) %reduce-scatter.7.cloned.1.call-update) | async-done | bytes 32784 | tf_op jit(solution)/shard_map/reduce_scatter | solution.py:62
  301.0 1.4 bitcast_subtract_fusion.5
  302.7 61.5 %all-gather.5.cloned.1.call-done = f32[2048,128]{1,0:T(8,128)} async-done(((f32[64,128]{1,0:T(8,128)}), f32[2048,128]{1,0:T(8,128)}) %all-gather.5.cloned.1.call-update) | async-done | bytes 1048592 | tf_op jit(solution)/shard_map/all_gather | solution.py:45
  364.2 3.4 fusion.20
  367.6 4.9 fusion.2
  372.6 2.9 copy.25
  375.5 2.4 fusion.10
  377.9 0.8 copy.15
  378.8 57.3 %reduce-scatter.9.cloned.1.call-done = f32[64,128]{1,0:T(8,128)} async-done(((f32[1024,128]{1,0:T(8,128)}), f32[64,128]{1,0:T(8,128)}) %reduce-scatter.9.cloned.1.call-update) | async-done | bytes 32784 | tf_op jit(solution)/shard_map/reduce_scatter | solution.py:49
  436.8 23.9 %all_gather.15 = f32[1024,128]{1,0:T(8,128)S(1)} all-gather(f32[64,128]{1,0:T(8,128)S(1)} %fusion.34), channel_id=1, replica_groups=mesh['row'=32,'col'=16] {'col'}, dimensions={0}, use_global_device_ids=true | all-gather | bytes 557056 | tf_op jit(solution)/shard_map/all_gather | solution.py:58
  460.7 2.1 fusion.24
  462.8 4.5 fusion
  467.3 2.9 copy.28
  470.2 2.4 fusion.8
  472.6 1.2 copy.16
  473.8 115.8 %reduce-scatter.11.cloned.1.call-done = f32[64,128]{1,0:T(8,128)} async-done(((f32[2048,128]{1,0:T(8,128)}), f32[64,128]{1,0:T(8,128)}) %reduce-scatter.11.cloned.1.call-update) | async-done | bytes 32784 | tf_op jit(solution)/shard_map/reduce_scatter | solution.py:62
  589.6 1.4 fusion.28
  (36 shorter events, 1.4 us)
Async XLA Ops:
  7.2 71.8 %copy-start = (f32[1,12,256,256]{3,2,1,0:T(8,128)S(1)}, f32[1,12,256,256]{3,2,1,0:T(8,128)}, u32[]{:S(2)}) copy-start(f32[1,12,256,256]{3,2,1,0:T(8,128)} %param.11) | copy-start | bytes 9437188
  7.2 68.4 %all-gather.3.cloned.1.call-start = ((), (), s32[]{:S(2)}) async-start(), calls=%async_computation.4 | async-start | bytes 1081344 | tf_op jit(solution)/shard_map/all_gather | solution.py:45
  8.8 138.7 %reduce-scatter.5.cloned.1.call-start = ((), (), s32[]{:S(2)}) async-start(), calls=%async_computation.5 | async-start | bytes 557056 | tf_op jit(solution)/shard_map/reduce_scatter | solution.py:49
  83.9 3.0 copy-start.9
  86.9 60.6 %copy-start.7 = (f32[1,64,128]{2,1,0:T(8,128)S(1)}, f32[1,64,128]{2,1,0:T(8,128)}, u32[]{:S(2)}) copy-start(f32[1,64,128]{2,1,0:T(8,128)} %param.18) | copy-start | bytes 98308
  86.9 60.6 %copy-start.8 = (f32[1,64,128]{2,1,0:T(8,128)S(1)}, f32[1,64,128]{2,1,0:T(8,128)}, u32[]{:S(2)}) copy-start(f32[1,64,128]{2,1,0:T(8,128)} %param.17) | copy-start | bytes 98308
  90.2 210.9 %reduce-scatter.7.cloned.1.call-start = ((), (), s32[]{:S(2)}) async-start(), calls=%async_computation.6 | async-start | bytes 1081344 | tf_op jit(solution)/shard_map/reduce_scatter | solution.py:62
  178.5 3.0 copy-start.10
  183.8 117.2 %copy-start.1 = (f32[1,64,128]{2,1,0:T(8,128)S(1)}, f32[1,64,128]{2,1,0:T(8,128)}, u32[]{:S(2)}) copy-start(f32[1,64,128]{2,1,0:T(8,128)} %param.15) | copy-start | bytes 98308
  183.8 117.2 %copy-start.2 = (f32[1,64,128]{2,1,0:T(8,128)S(1)}, f32[1,64,128]{2,1,0:T(8,128)}, u32[]{:S(2)}) copy-start(f32[1,64,128]{2,1,0:T(8,128)} %param.21) | copy-start | bytes 98308
  183.9 117.2 %copy-start.3 = (f32[1,64,128]{2,1,0:T(8,128)S(1)}, f32[1,64,128]{2,1,0:T(8,128)}, u32[]{:S(2)}) copy-start(f32[1,64,128]{2,1,0:T(8,128)} %param.20) | copy-start | bytes 98308
  183.9 117.2 %copy-start.4 = (f32[1,64,128]{2,1,0:T(8,128)S(1)}, f32[1,64,128]{2,1,0:T(8,128)}, u32[]{:S(2)}) copy-start(f32[1,64,128]{2,1,0:T(8,128)} %param.19) | copy-start | bytes 98308
  185.1 179.2 %all-gather.5.cloned.1.call-start = ((), (), s32[]{:S(2)}) async-start(), calls=%async_computation.7 | async-start | bytes 1081344 | tf_op jit(solution)/shard_map/all_gather | solution.py:45
  302.5 133.6 %reduce-scatter.9.cloned.1.call-start = ((), (), s32[]{:S(2)}) async-start(), calls=%async_computation.8 | async-start | bytes 557056 | tf_op jit(solution)/shard_map/reduce_scatter | solution.py:49
  378.7 210.8 %reduce-scatter.11.cloned.1.call-start = ((), (), s32[]{:S(2)}) async-start(), calls=%async_computation.9 | async-start | bytes 1081344 | tf_op jit(solution)/shard_map/reduce_scatter | solution.py:62
  436.8 30.4 %copy-start.6 = (f32[64,128]{1,0:T(8,128)}, f32[64,128]{1,0:T(8,128)S(1)}, u32[]{:S(2)}) copy-start(f32[64,128]{1,0:T(8,128)S(1)} %fusion.34) | copy-start | bytes 98308
  472.6 117.0 %copy-start.5 = (f32[64,128]{1,0:T(8,128)S(1)}, f32[64,128]{1,0:T(8,128)}, u32[]{:S(2)}) copy-start(f32[64,128]{1,0:T(8,128)} %reduce-scatter.7.cloned.1.call-done) | copy-start | bytes 98308
Sparse Core Ops, SparseCore 0:
  11.7 63.8 all-gather.2
  90.3 57.1 reduce-scatter.4
  185.2 115.7 reduce-scatter.6
  304.6 59.6 all-gather.4
  378.9 57.1 reduce-scatter.8
  473.9 115.5 reduce-scatter.10
where the time goes:
time: 599 us; the launch traced here: 598 us
  waiting for transfers between devices  474 us (79%)
  blocking collectives  47.5 us (8%)
  matrix products  39.3 us (7%)
  local copies, waits for them, and re-layouts  15.9 us (3%)
  between operations  14.9 us (2%)
    reduce_scatter x2, waiting for transfers between devices, on_device(): lax.psum_scatter(jnp.einsum('sc,sjb->cjb', col_pick, product, precision=h...  232 us
    all_gather x2, waiting for transfers between devices, on_device(): whole_cols = lax.all_gather(extrapolated, 'row', axis=0, tiled=True)  128 us
    reduce_scatter x2, waiting for transfers between devices, on_device(): lax.psum_scatter(jnp.einsum('sr,sib->rib', row_pick, forward_product, pre...  115 us
    all_gather x2, blocking collectives, on_device(): whole_rows = lax.all_gather(dual_vec, 'col', axis=0, tiled=True)  47.5 us
  transfers between devices with their start and end apart: 6, of which 6 were waited for; matrix products, arithmetic and copies ran while one was open for 0% of the time, Pallas kernels for 0%

commit v1 on v0

v1 whole, which is shorter than its diff:
```python
import functools

import jax
import jax.numpy as jnp
from jax import lax
from jax.experimental import pallas as pl
from jax.experimental.pallas import tpu as pltpu
from jax.sharding import PartitionSpec as P

MESH = pl.DeviceIdType.MESH
F32 = jnp.float32
BF16 = jnp.bfloat16

NX, NY, NZ = 4, 4, 16
RB_DEV = 4
CB_DEV = 8
SLOTS = 12
BS = 256
ITERS = 2
BATCH = 128
CHUNK = 64
HALF = CHUNK // 2
PARTS = BS // CHUNK

dual_step = 0.3
primal_step = 0.3

SIDES = (1, -1)
XY_PARTNERS = sorted(
    [(dx, dy) for dx in range(NX) for dy in range(NY) if (dx, dy) != (0, 0)],
    key=lambda d: -(min(d[0], NX - d[0]) + min(d[1], NY - d[1])),
)
FROM7, FROM6, FROM4, FROM8, FROM3, SUM5, SUM2, NEXT = range(8)
FIRST_HOPS = ((FROM8, 8, 3), (FROM7, 7, 2), (FROM6, 6, 1), (FROM4, 4, -1), (FROM3, 3, 1), (NEXT, 1, 1))


def split(value):
    high = value.astype(BF16)
    low = (value - high.astype(F32)).astype(BF16)
    return high, low


def kernel(
    rows_ref, cols_ref, live_ref,
    blocks_hbm, now_ref, prev_ref, dual_ref, bound_ref, cost_ref, lower_ref, upper_ref,
    primal_out, dual_out,
    place,
    blk, a_hi, a_lo, at_hi, at_lo,
    xg, xs, prod, ys, rz, dg, ds, zs, zc, rx, cur,
    blk_sem,
    xg_send, xg_recv, xc_send, xc_recv,
    rz_send, rz_recv, dg_send, dg_recv,
    zc_send, zc_recv, rx_send, rx_recv,
):
    row = lax.axis_index("row")
    z = lax.axis_index("col")
    x = row // (2 * NY)
    y = (row // 2) % NY
    core = row % 2
    other = 1 - core

    def wrap(value, size):
        return lax.rem(value + size, size)

    def plane(dx, dy):
        return (wrap(x + dx, NX) * (2 * NY) + wrap(y + dy, NY) * 2 + core, z)

    def along(dz):
        return (row, wrap(z + dz, NZ))

    sibling = (row + 1 - 2 * core, z)

    load = pltpu.make_async_copy(blocks_hbm, blk, blk_sem)
    load.start()

    barrier = pltpu.get_barrier_semaphore()
    greeted = [sibling] + [plane(dx, dy) for dx, dy in XY_PARTNERS]
    greeted += [along(sg * d) for d in (1, 2, 3, 5) for sg in SIDES]
    for device in greeted:
        pl.semaphore_signal(barrier, inc=1, device_id=device, device_id_type=MESH)
    pl.semaphore_wait(barrier, len(greeted))

    sends = []

    def send(src, dst, send_sem, recv_sem, device):
        copy = pltpu.make_async_remote_copy(
            src_ref=src, dst_ref=dst, send_sem=send_sem, recv_sem=recv_sem,
            device_id=device, device_id_type=MESH,
        )
        copy.start()
        sends.append(copy)
        return copy

    def gather_plane_start(it, value):
        own = xg.at[it, core, x, y]
        own[...] = value
        copies = {}
        for dx, dy in XY_PARTNERS:
            k = dx * NY + dy
            copies[dx, dy] = send(own, own, xg_send.at[it, k], xg_recv.at[it, k], plane(dx, dy))
        return copies

    def split_group(it, c, gx):
        for gy in range(NY):
            high, low = split(xg[it, c, gx, gy])
            at = gx * (2 * NY) + gy * 2 + c
            xs[at, :, :BATCH] = high
            xs[at, :, BATCH:] = low

    def gather_plane_finish(it, copies):
        forwards = []
        for dx in (0, 1, 3, 2):
            gx = wrap(x - dx, NX)
            for dy in range(NY):
                if (dx, dy) != (0, 0):
                    copies[dx, dy].wait_recv()
            group = xg.at[it, core, gx]
            forwards.append(send(group, group, xc_send.at[it, dx], xc_recv.at[it, dx], sibling))
            split_group(it, core, gx)
        for dx, copy in zip((0, 1, 3, 2), forwards):
            copy.wait_recv()
            split_group(it, other, wrap(x - dx, NX))

    def products(hi, lo, table, vec):
        for s in range(SLOTS):
            at = table[s]
            rhs = vec[pl.ds(at * PARTS, PARTS)].reshape(BS, 2 * BATCH)
            main = jnp.dot(hi[s], rhs, preferred_element_type=F32)
            rest = jnp.dot(lo[s], rhs[:, :BATCH], preferred_element_type=F32)
            prod[s] = (main[:, :BATCH] + main[:, BATCH:] + rest).reshape(PARTS, CHUNK, BATCH)

    def image_chunk(zd):
        r, part = zd // PARTS, zd % PARTS
        total = prod[place[r * CB_DEV], part]
        for c in range(1, CB_DEV):
            total += prod[place[r * CB_DEV + c], part]
        return total

    def adjoint_chunk(at):
        cb, part = at // PARTS, at % PARTS
        total = prod[place[cb], part]
        for r in range(1, RB_DEV):
            total += prod[place[r * CB_DEV + cb], part]
        return total

    def half(sg):
        return pl.ds(0 if sg == 1 else HALF, HALF)

    def reduce_ring(it):
        hops = {}
        for slot, far, via in FIRST_HOPS:
            for sg in SIDES:
                zd = wrap(z + sg * far, NZ)
                if not (slot == FROM8 and sg == -1):
                    ys[it, zd] = image_chunk(zd)
                src, dst = ys.at[it, zd], rz.at[it, (1 - sg) // 2, slot]
                if slot == FROM8:
                    src, dst = src.at[half(sg)], dst.at[half(sg)]
                sem = (it, (1 - sg) // 2, slot)
                hops[slot, sg] = send(src, dst, rz_send.at[sem], rz_recv.at[sem], along(sg * via))
        for far in (2, 5):
            for sg in SIDES:
                zd = wrap(z + sg * far, NZ)
                ys[it, zd] = image_chunk(zd)
        mine = image_chunk(z)
        for slot, far, parts in ((SUM5, 5, (FROM4, FROM6, FROM7, FROM8)), (SUM2, 2, (FROM3,))):
            for sg in SIDES:
                side = (1 - sg) // 2
                zd = wrap(z + sg * far, NZ)
                for part in parts:
                    hops[part, sg].wait_recv()
                    if part == FROM8:
                        ys[it, zd, half(sg)] += rz[it, side, part, half(sg)]
                    else:
                        ys[it, zd] += rz[it, side, part]
                sem = (it, side, slot)
                hops[slot, sg] = send(
                    ys.at[it, zd], rz.at[it, side, slot], rz_send.at[sem], rz_recv.at[sem], along(sg * far)
                )
        for slot in (NEXT, SUM2, SUM5):
            for sg in SIDES:
                hops[slot, sg].wait_recv()
                mine += rz[it, (1 - sg) // 2, slot]
        return mine

    def gather_ring(it, value):
        copies = {}

        def pass_on(far, via):
            at = wrap(z + via - far, NZ)
            ref = dg.at[it, at]
            sem = (it, far % NZ)
            if abs(far) == 8:
                sg = 1 if far == 8 else -1
                ref = ref.at[half(sg)]
                sem = (it, 8 if sg == 1 else 0)
            copies[far] = send(ref, ref, dg_send.at[sem], dg_recv.at[sem], along(via))

        def split_chunk(far):
            at = wrap(z - far, NZ)
            high, low = split(dg[it, at])
            ds[at, :, :BATCH] = high
            ds[at, :, BATCH:] = low

        dg[it, z] = value
        for far in (5, 2, 1):
            for sg in SIDES:
                pass_on(sg * far, sg * far)
        split_chunk(0)
        for sg in SIDES:
            copies[sg].wait_recv()
            split_chunk(sg)
        for sg in SIDES:
            copies[2 * sg].wait_recv()
            pass_on(3 * sg, sg)
            split_chunk(2 * sg)
        for sg in SIDES:
            copies[5 * sg].wait_recv()
            pass_on(8 * sg, 3 * sg)
            pass_on(7 * sg, 2 * sg)
            pass_on(6 * sg, sg)
            pass_on(4 * sg, -sg)
        for sg in SIDES:
            split_chunk(5 * sg)
        for far in (3, 4, 6, 7):
            for sg in SIDES:
                copies[sg * far].wait_recv()
                split_chunk(sg * far)
        copies[8].wait_recv()
        copies[-8].wait_recv()
        split_chunk(8)

    def reduce_plane(it):
        order = (2, 1, 3, 0)
        swaps = []
        for dx in order:
            gx = wrap(x + dx, NX)
            for gy in range(NY):
                zs[it, other, gx, gy] = adjoint_chunk(gx * (2 * NY) + gy * 2 + other)
            swaps.append(
                send(zs.at[it, other, gx], zc.at[it, gx], zc_send.at[it, dx], zc_recv.at[it, dx], sibling)
            )
        for dx in order:
            gx = wrap(x + dx, NX)
            for gy in range(NY):
                zs[it, core, gx, gy] = adjoint_chunk(gx * (2 * NY) + gy * 2 + core)
        copies = {}
        for dx, swap in zip(order, swaps):
            gx = wrap(x + dx, NX)
            swap.wait_recv()
            for dy in (2, 1, 3, 0):
                gy = wrap(y + dy, NY)
                zs[it, core, gx, gy] += zc[it, gx, gy]
                if (dx, dy) != (0, 0):
                    k = dx * NY + dy
                    copies[dx, dy] = send(
                        zs.at[it, core, gx, gy], rx.at[it, k], rx_send.at[it, k], rx_recv.at[it, k], plane(dx, dy)
                    )
        total = zs[it, core, x, y]
        for dx, dy in reversed(XY_PARTNERS):
            copies[dx, dy].wait_recv()
            total += rx[it, dx * NY + dy]
        return total

    gathers = gather_plane_start(0, 2.0 * now_ref[...] - prev_ref[...])
    cur[...] = now_ref[...]

    prod[SLOTS] = jnp.zeros((PARTS, CHUNK, BATCH), F32)
    live = live_ref[0, 0]
    keys = [
        jnp.where(s < live, rows_ref[0, s] * CB_DEV + cols_ref[0, s], -1) for s in range(SLOTS)
    ]
    for b in range(RB_DEV * CB_DEV):
        found = jnp.int32(SLOTS)
        for s in range(SLOTS):
            found = jnp.where(keys[s] == b, s, found)
        place[b] = found
    load.wait()

    def prepare(s, carry):
        value = blk[s]
        high, low = split(value)
        a_hi[s] = high
        a_lo[s] = low
        high, low = split(value.T)
        at_hi[s] = high
        at_lo[s] = low
        return carry

    lax.fori_loop(0, SLOTS, prepare, 0)

    dual = dual_ref[...]
    for it in range(ITERS):
        gather_plane_finish(it, gathers)
        products(a_hi, a_lo, [cols_ref[0, s] for s in range(SLOTS)], xs)
        image = reduce_ring(it)
        dual = jnp.maximum(dual + dual_step * (bound_ref[...] - image), 0.0)
        gather_ring(it, dual)
        products(at_hi, at_lo, [rows_ref[0, s] for s in range(SLOTS)], ds)
        adjoint = reduce_plane(it)
        before = cur[...]
        after = jnp.minimum(
            jnp.maximum(before - primal_step * (cost_ref[...] - adjoint), lower_ref[...]), upper_ref[...]
        )
        if it + 1 < ITERS:
            gathers = gather_plane_start(it + 1, 2.0 * after - before)
            cur[...] = after
        else:
            primal_out[...] = after
            dual_out[...] = dual
    for copy in sends:
        copy.wait_send()


def on_device(
    blocks, block_rows, block_cols, live_count, primal_now, primal_prev, dual_now, row_bound,
    objective, lower_bound, upper_bound,
):
    vmem = pl.BlockSpec(memory_space=pltpu.VMEM)
    smem = pl.BlockSpec(memory_space=pltpu.SMEM)
    dma = pltpu.SemaphoreType.DMA
    vec = jax.ShapeDtypeStruct((CHUNK, BATCH), F32)
    primal, dual = pl.pallas_call(
        kernel,
        out_shape=(vec, vec),
        in_specs=[smem] * 3 + [pl.BlockSpec(memory_space=pl.ANY)] + [vmem] * 7,
        out_specs=(vmem, vmem),
        scratch_shapes=[
            pltpu.SMEM((RB_DEV * CB_DEV,), jnp.int32),
            pltpu.VMEM((SLOTS, BS, BS), F32),
            pltpu.VMEM((SLOTS, BS, BS), BF16),
            pltpu.VMEM((SLOTS, BS, BS), BF16),
            pltpu.VMEM((SLOTS, BS, BS), BF16),
            pltpu.VMEM((SLOTS, BS, BS), BF16),
            pltpu.VMEM((ITERS, 2, NX, NY, CHUNK, BATCH), F32),
            pltpu.VMEM((2 * NX * NY, CHUNK, 2 * BATCH), BF16),
            pltpu.VMEM((SLOTS + 1, PARTS, CHUNK, BATCH), F32),
            pltpu.VMEM((ITERS, NZ, CHUNK, BATCH), F32),
            pltpu.VMEM((ITERS, 2, 8, CHUNK, BATCH), F32),
            pltpu.VMEM((ITERS, NZ, CHUNK, BATCH), F32),
            pltpu.VMEM((NZ, CHUNK, 2 * BATCH), BF16),
            pltpu.VMEM((ITERS, 2, NX, NY, CHUNK, BATCH), F32),
            pltpu.VMEM((ITERS, NX, NY, CHUNK, BATCH), F32),
            pltpu.VMEM((ITERS, NX * NY, CHUNK, BATCH), F32),
            pltpu.VMEM((CHUNK, BATCH), F32),
            dma,
            dma((ITERS, NX * NY)), dma((ITERS, NX * NY)),
            dma((ITERS, NX)), dma((ITERS, NX)),
            dma((ITERS, 2, 8)), dma((ITERS, 2, 8)),
            dma((ITERS, NZ)), dma((ITERS, NZ)),
            dma((ITERS, NX)), dma((ITERS, NX)),
            dma((ITERS, NX * NY)), dma((ITERS, NX * NY)),
        ],
        compiler_params=pltpu.CompilerParams(
            collective_id=0, has_side_effects=True, vmem_limit_bytes=48 * 1024 * 1024
        ),
        name="pdhg",
    )(
        block_rows, block_cols, live_count,
        blocks[0], primal_now[0], primal_prev[0], dual_now[0], row_bound[0],
        objective[0], lower_bound[0], upper_bound[0],
    )
    return (primal[None], dual[None])


def solution(mesh):
    in_specs = (
        P("row", "col", None, None),
        P("row", "col"),
        P("row", "col"),
        P("row", "col"),
        P("col", "row", None),
        P("col", "row", None),
        P("row", "col", None),
        P("row", "col", None),
        P("col", "row", None),
        P("col", "row", None),
        P("col", "row", None),
    )
    out_specs = (P("col", "row", None), P("row", "col", None))
    return jax.shard_map(
        on_device, mesh=mesh, in_specs=in_specs, out_specs=out_specs, check_vma=False
    )
```

time: 599 us -> 131 us (0.22)
  waiting for transfers between devices: 474 us -> 0 us
  Pallas kernels: 0 us -> 119 us
  blocking collectives: 47.5 us -> 0 us
  matrix products: 39.3 us -> 0 us
  between operations: 14.9 us -> 1.31 us
  local copies, waits for them, and re-layouts: 15.9 us -> 9.73 us
    reduce_scatter x4 -> x0, waiting for transfers between devices: 346 us -> none  [the longest x2 232 us: on_device(): lax.psum_scatter(jnp.einsum('sc,sjb->cjb', col_pick, product, precision=h...]
    all_gather x2 -> x0, waiting for transfers between devices: 128 us -> none  [on_device(): whole_cols = lax.all_gather(extrapolated, 'row', axis=0, tiled=True)]
    pallas_call x0 -> x1, Pallas kernels: none -> 119 us  [on_device(): pl.pallas_call(kernel, out_shape=(vec, vec), in_specs=[smem] * 3 + [pl.Bl...]
    all_gather x2 -> x0, blocking collectives: 47.5 us -> none  [on_device(): whole_rows = lax.all_gather(dual_vec, 'col', axis=0, tiled=True)]
    dot_general x12 -> x0, matrix products: 39.3 us -> none  [the longest x2 9.82 us: on_device(): jnp.einsum('sij,sjb->sib', tiles, forward_picked, precision=highest)]
    dot_general x8 -> x0, local copies, waits for them, and re-layouts: 15.8 us -> none  [the longest x2 5.9 us: on_device(): product = jnp.einsum('sij,sib->sjb', tiles, picked, precision=highest)]
    unnamed x22, local copies, waits for them, and re-layouts: 0.06 us -> 9.73 us
  transfers between devices with their start and end apart: 6 -> 0, of which waited for: 6 -> 0; matrix products, arithmetic and copies ran while one was open for 0% -> 0% of each run, Pallas kernels for 0% -> 0%
where the time goes in v1:
time: 131 us; the launch traced here: 130 us
  Pallas kernels  119 us (91%)
  local copies, waits for them, and re-layouts  9.73 us (7%)
  between operations  1.31 us (1%)
    pallas_call x1, Pallas kernels, on_device(): pl.pallas_call(kernel, out_shape=(vec, vec), in_specs=[smem] * 3 + [pl.Bl...  119 us
    unnamed x22, local copies, waits for them, and re-layouts  9.73 us

profile of v1, /device:TPU:1, one launch (start us, length us, event | category | flops | bytes accessed | tf_op | source)
XLA Modules:
  0.0 130.2 jit_solution(9340038298840707517)
XLA Ops:
  1.3 0.0 copy-start
  1.3 1.9 %copy-done = f32[1,12,256,256]{3,2,1,0:T(8,128)S(1)} copy-done((f32[1,12,256,256]{3,2,1,0:T(8,128)S(1)}, f32[1,12,256,256]{3,2,1,0:T(8,128)}, u32[]{:S(2)}) %copy-start) | copy-done | bytes 3145752
  3.2 0.0 copy-start.1
  3.2 0.8 copy-done.1
  3.9 0.0 copy-start.2
  3.9 0.8 copy-done.2
  4.7 0.0 copy-start.3
  4.7 0.8 copy-done.3
  5.4 0.0 copy-start.4
  5.4 0.8 copy-done.4
  6.2 0.0 copy-start.5
  6.2 0.8 copy-done.5
  7.0 0.0 copy-start.6
  7.0 0.8 copy-done.6
  7.7 0.0 copy-start.7
  7.7 0.8 copy-done.7
  8.5 0.0 copy-start.8
  8.5 0.7 copy-done.8
  9.1 0.0 copy-start.9
  9.1 0.7 copy-done.9
  9.8 119.1 %pdhg.1 = (f32[64,128]{1,0:T(8,128)S(1)}, f32[64,128]{1,0:T(8,128)S(1)}) custom-call(s32[1,12]{1,0:T(1,128)S(1)} %copy-done.8, s32[1,12]{1,0:T(1,128)S(1)} %copy-done.9, s32[1,1]{1,0:T(1,128)S(6)} %copy.15.live_ref, f32[12,256,256]{2,1,0:T(8,128)S(1)} %bitcast.10, f32[64,128]{1,0:T(8,128)S(1)} %bitcast.11, f32[64,128]{1,0:T(8,128)S(1)} %bitcast.12, ...), custom_call_target="tpu_custom_call" | custom-call | tf_op jit(solution)/shard_map/pdhg/pallas_call | solution.py:323
  128.9 0.6 copy.16
  129.5 0.6 copy.17
Async XLA Ops:
  1.3 1.9 %copy-start = (f32[1,12,256,256]{3,2,1,0:T(8,128)S(1)}, f32[1,12,256,256]{3,2,1,0:T(8,128)}, u32[]{:S(2)}) copy-start(f32[1,12,256,256]{3,2,1,0:T(8,128)} %param.11) | copy-start | bytes 9437188
  3.2 0.8 copy-start.1
  3.9 0.8 copy-start.2
  4.7 0.8 copy-start.3
  5.4 0.8 copy-start.4
  6.2 0.8 copy-start.5
  7.0 0.8 copy-start.6
  7.7 0.8 copy-start.7
  8.5 0.7 copy-start.8
  9.1 0.7 copy-start.9

commit v2 on v1

v2 whole, which is shorter than its diff:
```python
import functools

import jax
import jax.numpy as jnp
from jax import lax
from jax.experimental import pallas as pl
from jax.experimental.pallas import tpu as pltpu
from jax.sharding import PartitionSpec as P

MESH = pl.DeviceIdType.MESH
F32 = jnp.float32
BF16 = jnp.bfloat16

NX, NY, NZ = 4, 4, 16
RB_DEV = 4
CB_DEV = 8
SLOTS = 12
BS = 256
ITERS = 2
BATCH = 128
CHUNK = 64
HALF = CHUNK // 2
PARTS = BS // CHUNK

dual_step = 0.3
primal_step = 0.3

SIDES = (1, -1)
XY_PARTNERS = sorted(
    [(dx, dy) for dx in range(NX) for dy in range(NY) if (dx, dy) != (0, 0)],
    key=lambda d: -(min(d[0], NX - d[0]) + min(d[1], NY - d[1])),
)
FROM3, FROM4, FROM6, FROM7, FROM8, NEXT, SUM2, SUM5 = range(8)
FIRST_HOPS = ((FROM8, 8, 3), (FROM7, 7, 2), (FROM6, 6, 1), (FROM4, 4, -1), (FROM3, 3, 1), (NEXT, 1, 1))
SLOT_SUM = {FROM8: 0, FROM7: 0, FROM6: 0, FROM4: 0, FROM3: 1, NEXT: 2}
NOW, PREV, DUAL, BOUND, COST, LOWER, UPPER = range(7)


def split(value):
    high = value.astype(BF16)
    low = (value - high.astype(F32)).astype(BF16)
    return high, low


def kernel(
    rows_hbm, cols_hbm, live_hbm, blocks_hbm,
    now_hbm, prev_hbm, dual_hbm, bound_hbm, cost_hbm, lower_hbm, upper_hbm,
    primal_out, dual_out,
    rows_ref, cols_ref, live_ref, place,
    vecs, blk, a_hi, a_lo, at_hi, at_lo,
    xg, xs, prod, ys, rz, dg, ds, zs, zc, rx,
    blk_sem, list_sem, vec_sem,
    xg_send, xg_recv, xc_send, xc_recv,
    rz_send, rz_recv, dg_send, dg_recv,
    zc_send, zc_recv, rx_send, rx_recv,
):
    row = lax.axis_index("row")
    z = lax.axis_index("col")
    x = row // (2 * NY)
    y = (row // 2) % NY
    core = row % 2
    other = 1 - core

    def wrap(value, size):
        return lax.rem(value + size, size)

    def plane(dx, dy):
        return (wrap(x + dx, NX) * (2 * NY) + wrap(y + dy, NY) * 2 + core, z)

    def along(dz):
        return (row, wrap(z + dz, NZ))

    sibling = (row + 1 - 2 * core, z)

    barrier = pltpu.get_barrier_semaphore()
    greeted = [sibling] + [plane(dx, dy) for dx, dy in XY_PARTNERS]
    greeted += [along(sg * d) for d in (1, 2, 3, 5) for sg in SIDES]
    for device in greeted:
        pl.semaphore_signal(barrier, inc=1, device_id=device, device_id_type=MESH)

    vec_refs = (now_hbm, prev_hbm, dual_hbm, bound_hbm, cost_hbm, lower_hbm, upper_hbm)
    vec_loads = [pltpu.make_async_copy(ref, vecs.at[i], vec_sem.at[i]) for i, ref in enumerate(vec_refs)]
    list_loads = [
        pltpu.make_async_copy(src, dst, list_sem.at[i])
        for i, (src, dst) in enumerate(((rows_hbm, rows_ref), (cols_hbm, cols_ref), (live_hbm, live_ref)))
    ]
    load = pltpu.make_async_copy(blocks_hbm, blk, blk_sem)
    for copy in vec_loads[:2] + [load] + list_loads + vec_loads[2:]:
        copy.start()

    def send(src, dst, send_sem, recv_sem, device):
        copy = pltpu.make_async_remote_copy(
            src_ref=src, dst_ref=dst, send_sem=send_sem, recv_sem=recv_sem,
            device_id=device, device_id_type=MESH,
        )
        copy.start()
        return copy

    def waiter(ref, send_sem, recv_sem):
        return pltpu.make_async_remote_copy(
            src_ref=ref, dst_ref=ref, send_sem=send_sem, recv_sem=recv_sem,
            device_id=sibling, device_id_type=MESH,
        )

    def arrived(ref, recv_sem):
        waiter(ref, recv_sem, recv_sem).wait_recv()

    def half(h):
        return pl.ds(h * HALF, HALF)

    def gather_plane_start(it, h, value):
        own = xg.at[it, h, core, x, y]
        own[...] = value
        for dx, dy in XY_PARTNERS:
            send(own, own, xg_send.at[it, h], xg_recv.at[it, h, dx], plane(dx, dy))

    def split_group(it, h, c, gx):
        for gy in range(NY):
            high, low = split(xg[it, h, c, gx, gy])
            at = gx * (2 * NY) + gy * 2 + c
            xs[at, half(h), :BATCH] = high
            xs[at, half(h), BATCH:] = low

    def gather_plane_pass(it, h):
        for dx in (0, 1, 3, 2):
            gx = wrap(x - dx, NX)
            group = xg.at[it, h, core, gx]
            arrived(group if dx else group.at[pl.ds(0, NY - 1)], xg_recv.at[it, h, dx])
            send(group, group, xc_send.at[it, h], xc_recv.at[it, h, dx], sibling)
            split_group(it, h, core, gx)

    def gather_plane_last(it, h):
        for dx in (0, 1, 3, 2):
            gx = wrap(x - dx, NX)
            arrived(xg.at[it, h, other, gx], xc_recv.at[it, h, dx])
            split_group(it, h, other, gx)

    def products(hi, lo, table, vec):
        for s in range(SLOTS):
            at = table[s]
            rhs = vec[pl.ds(at * PARTS, PARTS)].reshape(BS, 2 * BATCH)
            main = jnp.dot(hi[s], rhs, preferred_element_type=F32)
            rest = jnp.dot(lo[s], rhs[:, :BATCH], preferred_element_type=F32)
            prod[s] = (main[:, :BATCH] + main[:, BATCH:] + rest).reshape(PARTS, 2, HALF, BATCH)

    def image_chunk(h, zd):
        r, part = zd // PARTS, zd % PARTS
        total = prod[place[r * CB_DEV], part, h]
        for c in range(1, CB_DEV):
            total += prod[place[r * CB_DEV + c], part, h]
        return total

    def adjoint_chunk(h, at):
        cb, part = at // PARTS, at % PARTS
        total = prod[place[cb], part, h]
        for r in range(1, RB_DEV):
            total += prod[place[r * CB_DEV + cb], part, h]
        return total

    def side(sg):
        return (1 - sg) // 2

    def has(h, sg, slot):
        return slot != FROM8 or side(sg) == h

    def ring_send(it, h):
        for slot, far, via in FIRST_HOPS:
            for sg in SIDES:
                if has(h, sg, slot):
                    zd = wrap(z + sg * far, NZ)
                    ys[it, h, zd] = image_chunk(h, zd)
                    to = SLOT_SUM[slot]
                    send(
                        ys.at[it, h, zd], rz.at[it, h, side(sg), slot],
                        rz_send.at[it, h], rz_recv.at[it, h, side(sg), to], along(sg * via),
                    )
        for far in (2, 5, 0):
            for sg in SIDES[: 2 if far else 1]:
                zd = wrap(z + sg * far, NZ)
                ys[it, h, zd] = image_chunk(h, zd)

    def ring_relay(it, h):
        for to, far, parts in ((1, 2, (FROM3,)), (0, 5, (FROM4, FROM6, FROM7, FROM8))):
            for sg in SIDES:
                zd = wrap(z + sg * far, NZ)
                parts_here = [part for part in parts if has(h, sg, part)]
                first, count = parts_here[0], len(parts_here)
                arrived(rz.at[it, h, side(sg), pl.ds(first, count)], rz_recv.at[it, h, side(sg), to])
                total = ys[it, h, zd]
                for part in parts_here:
                    total += rz[it, h, side(sg), part]
                ys[it, h, zd] = total
                slot = SUM5 if far == 5 else SUM2
                send(
                    ys.at[it, h, zd], rz.at[it, h, side(sg), slot],
                    rz_send.at[it, h], rz_recv.at[it, h, side(sg), 2], along(sg * far),
                )

    def ring_sum(it, h):
        total = ys[it, h, z]
        for sg in SIDES:
            arrived(rz.at[it, h, side(sg), pl.ds(NEXT, 3)], rz_recv.at[it, h, side(sg), 2])
            for slot in (NEXT, SUM2, SUM5):
                total += rz[it, h, side(sg), slot]
        return total

    def ring_pass(it, h, far, via):
        ref = dg.at[it, h, wrap(z + via - far, NZ)]
        sem = far % NZ if abs(far) in (1, 2, 5) else 0
        send(ref, ref, dg_send.at[it, h], dg_recv.at[it, h, sem], along(via))

    def ring_split(it, h, far):
        at = wrap(z - far, NZ)
        high, low = split(dg[it, h, at])
        ds[at, half(h), :BATCH] = high
        ds[at, half(h), BATCH:] = low

    def ring_arrived(it, h, far):
        arrived(dg.at[it, h, 0], dg_recv.at[it, h, far % NZ])

    def gather_ring_start(it, h, value):
        dg[it, h, z] = value
        for far in (5, 2, 1):
            for sg in SIDES:
                ring_pass(it, h, sg * far, sg * far)
        ring_split(it, h, 0)

    def gather_ring_relay(it, h):
        for sg in SIDES:
            ring_arrived(it, h, 2 * sg)
            ring_pass(it, h, 3 * sg, sg)
        for sg in SIDES:
            ring_arrived(it, h, 5 * sg)
            if has(h, sg, FROM8):
                ring_pass(it, h, 8 * sg, 3 * sg)
            ring_pass(it, h, 7 * sg, 2 * sg)
            ring_pass(it, h, 6 * sg, sg)
            ring_pass(it, h, 4 * sg, -sg)
        for sg in SIDES:
            ring_arrived(it, h, sg)
            for far in (1, 2, 5):
                ring_split(it, h, far * sg)

    def gather_ring_finish(it, h):
        arrived(dg.at[it, h, pl.ds(0, 9)], dg_recv.at[it, h, 0])
        for far in (3, 4, 6, 7):
            for sg in SIDES:
                ring_split(it, h, sg * far)
        ring_split(it, h, 8)

    plane_order = (2, 1, 3, 0)

    def plane_swap(it, h):
        for dx in plane_order:
            gx = wrap(x + dx, NX)
            for gy in range(NY):
                zs[it, h, other, gx, gy] = adjoint_chunk(h, gx * (2 * NY) + gy * 2 + other)
            send(
                zs.at[it, h, other, gx], zc.at[it, h, gx],
                zc_send.at[it, h], zc_recv.at[it, h, dx], sibling,
            )

    def plane_send(it, h):
        for dx in plane_order:
            gx = wrap(x + dx, NX)
            for gy in range(NY):
                zs[it, h, core, gx, gy] = adjoint_chunk(h, gx * (2 * NY) + gy * 2 + core)
        for dx in plane_order:
            gx = wrap(x + dx, NX)
            arrived(zc.at[it, h, gx], zc_recv.at[it, h, dx])
            for dy in (2, 1, 3, 0):
                gy = wrap(y + dy, NY)
                zs[it, h, core, gx, gy] += zc[it, h, gx, gy]
                if (dx, dy) != (0, 0):
                    send(
                        zs.at[it, h, core, gx, gy], rx.at[it, h, dx * NY + dy - 1],
                        rx_send.at[it, h], rx_recv.at[it, h], plane(dx, dy),
                    )

    def plane_sum(it, h):
        total = zs[it, h, core, x, y]
        arrived(rx.at[it, h], rx_recv.at[it, h])
        for k in range(NX * NY - 1):
            total += rx[it, h, k]
        return total

    for copy in vec_loads[:2]:
        copy.wait()
    pl.semaphore_wait(barrier, len(greeted))
    for h in range(2):
        gather_plane_start(0, h, 2.0 * vecs[NOW, half(h)] - vecs[PREV, half(h)])

    prod[SLOTS] = jnp.zeros((PARTS, 2, HALF, BATCH), F32)
    for copy in list_loads + vec_loads[2:]:
        copy.wait()
    live = live_ref[0, 0]
    keys = [
        jnp.where(s < live, rows_ref[0, s] * CB_DEV + cols_ref[0, s], -1) for s in range(SLOTS)
    ]
    for b in range(RB_DEV * CB_DEV):
        found = jnp.int32(SLOTS)
        for s in range(SLOTS):
            found = jnp.where(keys[s] == b, s, found)
        place[b] = found
    load.wait()

    def prepare(s, carry):
        value = blk[s]
        high, low = split(value)
        a_hi[s] = high
        a_lo[s] = low
        high, low = split(value.T)
        at_hi[s] = high
        at_lo[s] = low
        return carry

    lax.fori_loop(0, SLOTS, prepare, 0)

    for it in range(ITERS):
        for h in range(2):
            gather_plane_pass(it, h)
        for h in range(2):
            gather_plane_last(it, h)
        products(a_hi, a_lo, [cols_ref[0, s] for s in range(SLOTS)], xs)
        for h in range(2):
            ring_send(it, h)
        for h in range(2):
            ring_relay(it, h)
        for h in range(2):
            image = ring_sum(it, h)
            dual = jnp.maximum(vecs[DUAL, half(h)] + dual_step * (vecs[BOUND, half(h)] - image), 0.0)
            vecs[DUAL, half(h)] = dual
            gather_ring_start(it, h, dual)
        for h in range(2):
            gather_ring_relay(it, h)
        for h in range(2):
            gather_ring_finish(it, h)
        products(at_hi, at_lo, [rows_ref[0, s] for s in range(SLOTS)], ds)
        for h in range(2):
            plane_swap(it, h)
        for h in range(2):
            plane_send(it, h)
        for h in range(2):
            adjoint = plane_sum(it, h)
            before = vecs[NOW, half(h)]
            after = jnp.minimum(
                jnp.maximum(before - primal_step * (vecs[COST, half(h)] - adjoint), vecs[LOWER, half(h)]),
                vecs[UPPER, half(h)],
            )
            if it + 1 < ITERS:
                gather_plane_start(it + 1, h, 2.0 * after - before)
                vecs[NOW, half(h)] = after
            else:
                primal_out[half(h), :] = after
                dual_out[half(h), :] = vecs[DUAL, half(h)]
    for it in range(ITERS):
        for h in range(2):
            direct = rx.at[it, h]
            for sem in (xg_send, rz_send, dg_send, rx_send):
                waiter(direct, sem.at[it, h], sem.at[it, h]).wait_send()
            for sem in (xc_send, zc_send):
                waiter(zc.at[it, h], sem.at[it, h], sem.at[it, h]).wait_send()


def on_device(
    blocks, block_rows, block_cols, live_count, primal_now, primal_prev, dual_now, row_bound,
    objective, lower_bound, upper_bound,
):
    vmem = pl.BlockSpec(memory_space=pltpu.VMEM)
    dma = pltpu.SemaphoreType.DMA
    vec = jax.ShapeDtypeStruct((CHUNK, BATCH), F32)
    primal, dual = pl.pallas_call(
        kernel,
        out_shape=(vec, vec),
        in_specs=[pl.BlockSpec(memory_space=pl.ANY)] * 11,
        out_specs=(vmem, vmem),
        scratch_shapes=[
            pltpu.SMEM((1, SLOTS), jnp.int32),
            pltpu.SMEM((1, SLOTS), jnp.int32),
            pltpu.SMEM((1, 1), jnp.int32),
            pltpu.SMEM((RB_DEV * CB_DEV,), jnp.int32),
            pltpu.VMEM((7, CHUNK, BATCH), F32),
            pltpu.VMEM((SLOTS, BS, BS), F32),
            pltpu.VMEM((SLOTS, BS, BS), BF16),
            pltpu.VMEM((SLOTS, BS, BS), BF16),
            pltpu.VMEM((SLOTS, BS, BS), BF16),
            pltpu.VMEM((SLOTS, BS, BS), BF16),
            pltpu.VMEM((ITERS, 2, 2, NX, NY, HALF, BATCH), F32),
            pltpu.VMEM((2 * NX * NY, CHUNK, 2 * BATCH), BF16),
            pltpu.VMEM((SLOTS + 1, PARTS, 2, HALF, BATCH), F32),
            pltpu.VMEM((ITERS, 2, NZ, HALF, BATCH), F32),
            pltpu.VMEM((ITERS, 2, 2, 8, HALF, BATCH), F32),
            pltpu.VMEM((ITERS, 2, NZ, HALF, BATCH), F32),
            pltpu.VMEM((NZ, CHUNK, 2 * BATCH), BF16),
            pltpu.VMEM((ITERS, 2, 2, NX, NY, HALF, BATCH), F32),
            pltpu.VMEM((ITERS, 2, NX, NY, HALF, BATCH), F32),
            pltpu.VMEM((ITERS, 2, NX * NY - 1, HALF, BATCH), F32),
            dma, dma((3,)), dma((7,)),
            dma((ITERS, 2)), dma((ITERS, 2, NX)),
            dma((ITERS, 2)), dma((ITERS, 2, NX)),
            dma((ITERS, 2)), dma((ITERS, 2, 2, 3)),
            dma((ITERS, 2)), dma((ITERS, 2, NZ)),
            dma((ITERS, 2)), dma((ITERS, 2, NX)),
            dma((ITERS, 2)), dma((ITERS, 2)),
        ],
        compiler_params=pltpu.CompilerParams(
            collective_id=0, has_side_effects=True, vmem_limit_bytes=56 * 1024 * 1024
        ),
        name="pdhg",
    )(
        block_rows, block_cols, live_count, blocks[0],
        primal_now[0], primal_prev[0], dual_now[0], row_bound[0],
        objective[0], lower_bound[0], upper_bound[0],
    )
    return (primal[None], dual[None])


def solution(mesh):
    in_specs = (
        P("row", "col", None, None),
        P("row", "col"),
        P("row", "col"),
        P("row", "col"),
        P("col", "row", None),
        P("col", "row", None),
        P("row", "col", None),
        P("row", "col", None),
        P("col", "row", None),
        P("col", "row", None),
        P("col", "row", None),
    )
    out_specs = (P("col", "row", None), P("row", "col", None))
    return jax.shard_map(
        on_device, mesh=mesh, in_specs=in_specs, out_specs=out_specs, check_vma=False
    )
```

time: 131 us -> 113 us (0.86)
  Pallas kernels: 119 us -> 109 us
  local copies, waits for them, and re-layouts: 9.73 us -> 2.75 us
    pallas_call x1, Pallas kernels: 119 us -> 109 us  [on_device(): pl.pallas_call(kernel, out_shape=(vec, vec), in_specs=[pl.BlockSpec(memor...]
    unnamed x22 -> x2, local copies, waits for them, and re-layouts: 9.73 us -> 2.75 us
where the time goes in v2:
time: 113 us
  Pallas kernels  109 us (96%)
  local copies, waits for them, and re-layouts  2.75 us (2%)
  between operations  1.29 us (1%)
    pallas_call x1, Pallas kernels, on_device(): pl.pallas_call(kernel, out_shape=(vec, vec), in_specs=[pl.BlockSpec(memor...  109 us
    unnamed x2, local copies, waits for them, and re-layouts  2.75 us

profile of v2, /device:TPU:1, one launch (start us, length us, event | category | flops | bytes accessed | tf_op | source)
XLA Modules:
  0.0 112.6 jit_solution(864538103361896610)
XLA Ops:
  1.3 108.6 %pdhg.1 = (f32[64,128]{1,0:T(8,128)}, f32[64,128]{1,0:T(8,128)}) custom-call(s32[1,12]{1,0:T(1,128)} %rows_hbm.1, s32[1,12]{1,0:T(1,128)} %cols_hbm.1, s32[1,1]{1,0:T(1,128)S(6)} %copy.15.live_hbm, f32[12,256,256]{2,1,0:T(8,128)} %bitcast.10, f32[64,128]{1,0:T(8,128)} %bitcast.11, f32[64,128]{1,0:T(8,128)} %bitcast.12, f32[64,128]{1,0:T(8,128)} %bitcast.13, ...), custom_call_target="tpu_custom_call" | custom-call | tf_op jit(solution)/shard_map/pdhg/pallas_call | solution.py:372
  109.9 1.4 %copy.16 = f32[1,64,128]{2,1,0:T(8,128)} copy(f32[1,64,128]{2,1,0:T(8,128)} %bitcast.19) | data formatting | bytes 65536
  111.2 1.4 %copy.17 = f32[1,64,128]{2,1,0:T(8,128)} copy(f32[1,64,128]{2,1,0:T(8,128)} %bitcast.18) | data formatting | bytes 65536

commit v3 on v2

--- a/solution.py
+++ b/solution.py
@@ -19,7 +19,8 @@
 ITERS = 2
 BATCH = 128
 CHUNK = 64
-HALF = CHUNK // 2
+CUTS = 2
+ROWS = CHUNK // CUTS
 PARTS = BS // CHUNK
 
 dual_step = 0.3
@@ -45,7 +46,7 @@
 def kernel(
     rows_hbm, cols_hbm, live_hbm, blocks_hbm,
     now_hbm, prev_hbm, dual_hbm, bound_hbm, cost_hbm, lower_hbm, upper_hbm,
-    primal_out, dual_out,
+    result,
     rows_ref, cols_ref, live_ref, place,
     vecs, blk, a_hi, a_lo, at_hi, at_lo,
     xg, xs, prod, ys, rz, dg, ds, zs, zc, rx,
@@ -105,8 +106,8 @@
     def arrived(ref, recv_sem):
         waiter(ref, recv_sem, recv_sem).wait_recv()
 
-    def half(h):
-        return pl.ds(h * HALF, HALF)
+    def rows_of(h):
+        return pl.ds(h * ROWS, ROWS)
 
     def gather_plane_start(it, h, value):
         own = xg.at[it, h, core, x, y]
@@ -118,8 +119,8 @@
         for gy in range(NY):
             high, low = split(xg[it, h, c, gx, gy])
             at = gx * (2 * NY) + gy * 2 + c
-            xs[at, half(h), :BATCH] = high
-            xs[at, half(h), BATCH:] = low
+            xs[at, rows_of(h), :BATCH] = high
+            xs[at, rows_of(h), BATCH:] = low
 
     def gather_plane_pass(it, h):
         for dx in (0, 1, 3, 2):
@@ -141,43 +142,42 @@
             rhs = vec[pl.ds(at * PARTS, PARTS)].reshape(BS, 2 * BATCH)
             main = jnp.dot(hi[s], rhs, preferred_element_type=F32)
             rest = jnp.dot(lo[s], rhs[:, :BATCH], preferred_element_type=F32)
-            prod[s] = (main[:, :BATCH] + main[:, BATCH:] + rest).reshape(PARTS, 2, HALF, BATCH)
-
-    def image_chunk(h, zd):
-        r, part = zd // PARTS, zd % PARTS
-        total = prod[place[r * CB_DEV], part, h]
-        for c in range(1, CB_DEV):
-            total += prod[place[r * CB_DEV + c], part, h]
-        return total
-
-    def adjoint_chunk(h, at):
-        cb, part = at // PARTS, at % PARTS
-        total = prod[place[cb], part, h]
-        for r in range(1, RB_DEV):
-            total += prod[place[r * CB_DEV + cb], part, h]
-        return total
+            prod[s] = (main[:, :BATCH] + main[:, BATCH:] + rest).reshape(PARTS, CUTS, ROWS, BATCH)
+
+    def image_sums(it):
+        for r in range(RB_DEV):
+            total = prod[place[r * CB_DEV]]
+            for c in range(1, CB_DEV):
+                total += prod[place[r * CB_DEV + c]]
+            ys[it, r * PARTS : (r + 1) * PARTS] = total
+
+    def adjoint_sums(it):
+        for cb in range(CB_DEV):
+            total = prod[place[cb]]
+            for r in range(1, RB_DEV):
+                total += prod[place[r * CB_DEV + cb]]
+            for part in range(PARTS):
+                at = cb * PARTS + part
+                gx, gy, c = at // (2 * NY), at // 2 % NY, at % 2
+                for h in range(CUTS):
+                    zs[it, h, c, gx, gy] = total[part, h]
 
     def side(sg):
         return (1 - sg) // 2
 
     def has(h, sg, slot):
-        return slot != FROM8 or side(sg) == h
+        return slot != FROM8 or side(sg) == h % 2
 
     def ring_send(it, h):
         for slot, far, via in FIRST_HOPS:
             for sg in SIDES:
                 if has(h, sg, slot):
                     zd = wrap(z + sg * far, NZ)
-                    ys[it, h, zd] = image_chunk(h, zd)
                     to = SLOT_SUM[slot]
                     send(
-                        ys.at[it, h, zd], rz.at[it, h, side(sg), slot],
+                        ys.at[it, zd, h], rz.at[it, h, side(sg), slot],
                         rz_send.at[it, h], rz_recv.at[it, h, side(sg), to], along(sg * via),
                     )
-        for far in (2, 5, 0):
-            for sg in SIDES[: 2 if far else 1]:
-                zd = wrap(z + sg * far, NZ)
-                ys[it, h, zd] = image_chunk(h, zd)
 
     def ring_relay(it, h):
         for to, far, parts in ((1, 2, (FROM3,)), (0, 5, (FROM4, FROM6, FROM7, FROM8))):
@@ -186,18 +186,18 @@
                 parts_here = [part for part in parts if has(h, sg, part)]
                 first, count = parts_here[0], len(parts_here)
                 arrived(rz.at[it, h, side(sg), pl.ds(first, count)], rz_recv.at[it, h, side(sg), to])
-                total = ys[it, h, zd]
+                total = ys[it, zd, h]
                 for part in parts_here:
                     total += rz[it, h, side(sg), part]
-                ys[it, h, zd] = total
+                ys[it, zd, h] = total
                 slot = SUM5 if far == 5 else SUM2
                 send(
-                    ys.at[it, h, zd], rz.at[it, h, side(sg), slot],
+                    ys.at[it, zd, h], rz.at[it, h, side(sg), slot],
                     rz_send.at[it, h], rz_recv.at[it, h, side(sg), 2], along(sg * far),
                 )
 
     def ring_sum(it, h):
-        total = ys[it, h, z]
+        total = ys[it, z, h]
         for sg in SIDES:
             arrived(rz.at[it, h, side(sg), pl.ds(NEXT, 3)], rz_recv.at[it, h, side(sg), 2])
             for slot in (NEXT, SUM2, SUM5):
@@ -212,8 +212,8 @@
     def ring_split(it, h, far):
         at = wrap(z - far, NZ)
         high, low = split(dg[it, h, at])
-        ds[at, half(h), :BATCH] = high
-        ds[at, half(h), BATCH:] = low
+        ds[at, rows_of(h), :BATCH] = high
+        ds[at, rows_of(h), BATCH:] = low
 
     def ring_arrived(it, h, far):
         arrived(dg.at[it, h, 0], dg_recv.at[it, h, far % NZ])
@@ -253,8 +253,6 @@
     def plane_swap(it, h):
         for dx in plane_order:
             gx = wrap(x + dx, NX)
-            for gy in range(NY):
-                zs[it, h, other, gx, gy] = adjoint_chunk(h, gx * (2 * NY) + gy * 2 + other)
             send(
                 zs.at[it, h, other, gx], zc.at[it, h, gx],
                 zc_send.at[it, h], zc_recv.at[it, h, dx], sibling,
@@ -263,17 +261,12 @@
     def plane_send(it, h):
         for dx in plane_order:
             gx = wrap(x + dx, NX)
-            for gy in range(NY):
-                zs[it, h, core, gx, gy] = adjoint_chunk(h, gx * (2 * NY) + gy * 2 + core)
-        for dx in plane_order:
-            gx = wrap(x + dx, NX)
             arrived(zc.at[it, h, gx], zc_recv.at[it, h, dx])
+            zs[it, h, core, gx] += zc[it, h, gx]
             for dy in (2, 1, 3, 0):
-                gy = wrap(y + dy, NY)
-                zs[it, h, core, gx, gy] += zc[it, h, gx, gy]
                 if (dx, dy) != (0, 0):
                     send(
-                        zs.at[it, h, core, gx, gy], rx.at[it, h, dx * NY + dy - 1],
+                        zs.at[it, h, core, gx, wrap(y + dy, NY)], rx.at[it, h, dx * NY + dy - 1],
                         rx_send.at[it, h], rx_recv.at[it, h], plane(dx, dy),
                     )
 
@@ -287,10 +280,10 @@
     for copy in vec_loads[:2]:
         copy.wait()
     pl.semaphore_wait(barrier, len(greeted))
-    for h in range(2):
-        gather_plane_start(0, h, 2.0 * vecs[NOW, half(h)] - vecs[PREV, half(h)])
-
-    prod[SLOTS] = jnp.zeros((PARTS, 2, HALF, BATCH), F32)
+    for h in range(CUTS):
+        gather_plane_start(0, h, 2.0 * vecs[NOW, rows_of(h)] - vecs[PREV, rows_of(h)])
+
+    prod[SLOTS] = jnp.zeros((PARTS, CUTS, ROWS, BATCH), F32)
     for copy in list_loads + vec_loads[2:]:
         copy.wait()
     live = live_ref[0, 0]
@@ -317,45 +310,47 @@
     lax.fori_loop(0, SLOTS, prepare, 0)
 
     for it in range(ITERS):
-        for h in range(2):
+        for h in range(CUTS):
             gather_plane_pass(it, h)
-        for h in range(2):
+        for h in range(CUTS):
             gather_plane_last(it, h)
         products(a_hi, a_lo, [cols_ref[0, s] for s in range(SLOTS)], xs)
-        for h in range(2):
+        image_sums(it)
+        for h in range(CUTS):
             ring_send(it, h)
-        for h in range(2):
+        for h in range(CUTS):
             ring_relay(it, h)
-        for h in range(2):
+        for h in range(CUTS):
             image = ring_sum(it, h)
-            dual = jnp.maximum(vecs[DUAL, half(h)] + dual_step * (vecs[BOUND, half(h)] - image), 0.0)
-            vecs[DUAL, half(h)] = dual
+            dual = jnp.maximum(vecs[DUAL, rows_of(h)] + dual_step * (vecs[BOUND, rows_of(h)] - image), 0.0)
+            vecs[DUAL, rows_of(h)] = dual
             gather_ring_start(it, h, dual)
-        for h in range(2):
+        for h in range(CUTS):
             gather_ring_relay(it, h)
-        for h in range(2):
+        for h in range(CUTS):
             gather_ring_finish(it, h)
         products(at_hi, at_lo, [rows_ref[0, s] for s in range(SLOTS)], ds)
-        for h in range(2):
+        adjoint_sums(it)
+        for h in range(CUTS):
             plane_swap(it, h)
-        for h in range(2):
+        for h in range(CUTS):
             plane_send(it, h)
-        for h in range(2):
+        for h in range(CUTS):
             adjoint = plane_sum(it, h)
-            before = vecs[NOW, half(h)]
+            before = vecs[NOW, rows_of(h)]
             after = jnp.minimum(
-                jnp.maximum(before - primal_step * (vecs[COST, half(h)] - adjoint), vecs[LOWER, half(h)]),
-                vecs[UPPER, half(h)],
+                jnp.maximum(before - primal_step * (vecs[COST, rows_of(h)] - adjoint), vecs[LOWER, rows_of(h)]),
+                vecs[UPPER, rows_of(h)],
             )
             if it + 1 < ITERS:
                 gather_plane_start(it + 1, h, 2.0 * after - before)
-                vecs[NOW, half(h)] = after
+                vecs[NOW, rows_of(h)] = after
             else:
-                primal_out[half(h), :] = after
-                dual_out[half(h), :] = vecs[DUAL, half(h)]
+                result[0, rows_of(h), :] = after
+                result[1, rows_of(h), :] = vecs[DUAL, rows_of(h)]
     for it in range(ITERS):
-        for h in range(2):
-            direct = rx.at[it, h]
+        for h in range(CUTS):
+            direct = dg.at[it, h, pl.ds(0, NZ - 1)]
             for sem in (xg_send, rz_send, dg_send, rx_send):
                 waiter(direct, sem.at[it, h], sem.at[it, h]).wait_send()
             for sem in (xc_send, zc_send):
@@ -368,12 +363,11 @@
 ):
     vmem = pl.BlockSpec(memory_space=pltpu.VMEM)
     dma = pltpu.SemaphoreType.DMA
-    vec = jax.ShapeDtypeStruct((CHUNK, BATCH), F32)
-    primal, dual = pl.pallas_call(
+    result = pl.pallas_call(
         kernel,
-        out_shape=(vec, vec),
+        out_shape=jax.ShapeDtypeStruct((2, CHUNK, BATCH), F32),
         in_specs=[pl.BlockSpec(memory_space=pl.ANY)] * 11,
-        out_specs=(vmem, vmem),
+        out_specs=vmem,
         scratch_shapes=[
             pltpu.SMEM((1, SLOTS), jnp.int32),
             pltpu.SMEM((1, SLOTS), jnp.int32),
@@ -385,23 +379,23 @@
             pltpu.VMEM((SLOTS, BS, BS), BF16),
             pltpu.VMEM((SLOTS, BS, BS), BF16),
             pltpu.VMEM((SLOTS, BS, BS), BF16),
-            pltpu.VMEM((ITERS, 2, 2, NX, NY, HALF, BATCH), F32),
+            pltpu.VMEM((ITERS, CUTS, 2, NX, NY, ROWS, BATCH), F32),
             pltpu.VMEM((2 * NX * NY, CHUNK, 2 * BATCH), BF16),
-            pltpu.VMEM((SLOTS + 1, PARTS, 2, HALF, BATCH), F32),
-            pltpu.VMEM((ITERS, 2, NZ, HALF, BATCH), F32),
-            pltpu.VMEM((ITERS, 2, 2, 8, HALF, BATCH), F32),
-            pltpu.VMEM((ITERS, 2, NZ, HALF, BATCH), F32),
+            pltpu.VMEM((SLOTS + 1, PARTS, CUTS, ROWS, BATCH), F32),
+            pltpu.VMEM((ITERS, NZ, CUTS, ROWS, BATCH), F32),
+            pltpu.VMEM((ITERS, CUTS, 2, 8, ROWS, BATCH), F32),
+            pltpu.VMEM((ITERS, CUTS, NZ, ROWS, BATCH), F32),
             pltpu.VMEM((NZ, CHUNK, 2 * BATCH), BF16),
-            pltpu.VMEM((ITERS, 2, 2, NX, NY, HALF, BATCH), F32),
-            pltpu.VMEM((ITERS, 2, NX, NY, HALF, BATCH), F32),
-            pltpu.VMEM((ITERS, 2, NX * NY - 1, HALF, BATCH), F32),
+            pltpu.VMEM((ITERS, CUTS, 2, NX, NY, ROWS, BATCH), F32),
+            pltpu.VMEM((ITERS, CUTS, NX, NY, ROWS, BATCH), F32),
+            pltpu.VMEM((ITERS, CUTS, NX * NY - 1, ROWS, BATCH), F32),
             dma, dma((3,)), dma((7,)),
-            dma((ITERS, 2)), dma((ITERS, 2, NX)),
-            dma((ITERS, 2)), dma((ITERS, 2, NX)),
-            dma((ITERS, 2)), dma((ITERS, 2, 2, 3)),
-            dma((ITERS, 2)), dma((ITERS, 2, NZ)),
-            dma((ITERS, 2)), dma((ITERS, 2, NX)),
-            dma((ITERS, 2)), dma((ITERS, 2)),
+            dma((ITERS, CUTS)), dma((ITERS, CUTS, NX)),
+            dma((ITERS, CUTS)), dma((ITERS, CUTS, NX)),
+            dma((ITERS, CUTS)), dma((ITERS, CUTS, 2, 3)),
+            dma((ITERS, CUTS)), dma((ITERS, CUTS, NZ)),
+            dma((ITERS, CUTS)), dma((ITERS, CUTS, NX)),
+            dma((ITERS, CUTS)), dma((ITERS, CUTS)),
         ],
         compiler_params=pltpu.CompilerParams(
             collective_id=0, has_side_effects=True, vmem_limit_bytes=56 * 1024 * 1024
@@ -412,7 +406,7 @@
         primal_now[0], primal_prev[0], dual_now[0], row_bound[0],
         objective[0], lower_bound[0], upper_bound[0],
     )
-    return (primal[None], dual[None])
+    return (result[:1], result[1:])
 
 
 def solution(mesh):

time: 113 us -> 113 us (level)
  local copies, waits for them, and re-layouts: 2.75 us -> 1.4 us
    unnamed x2 -> x0, local copies, waits for them, and re-layouts: 2.75 us -> none
    slice x0 -> x1, local copies, waits for them, and re-layouts: none -> 1.4 us  [on_device(): return (result[:1], result[1:])]
    pallas_call x1, Pallas kernels: 109 us -> 110 us  [on_device(): pl.pallas_call(kernel, out_shape=jax.ShapeDtypeStruct((2, CHUNK, BATCH),...]
where the time goes in v3:
time: 113 us; the launch traced here: 112 us
  Pallas kernels  110 us (97%)
  local copies, waits for them, and re-layouts  1.4 us (1%)
  between operations  1.29 us (1%)
    pallas_call x1, Pallas kernels, on_device(): pl.pallas_call(kernel, out_shape=jax.ShapeDtypeStruct((2, CHUNK, BATCH),...  110 us

profile of v3, /device:TPU:1, one launch (start us, length us, event | category | flops | bytes accessed | tf_op | source)
XLA Modules:
  0.0 112.4 jit_solution(18433181788956939518)
XLA Ops:
  1.3 109.7 %pdhg.1 = f32[2,64,128]{2,1,0:T(8,128)} custom-call(s32[1,12]{1,0:T(1,128)} %rows_hbm.1, s32[1,12]{1,0:T(1,128)} %cols_hbm.1, s32[1,1]{1,0:T(1,128)S(6)} %copy.13.live_hbm, f32[12,256,256]{2,1,0:T(8,128)} %bitcast.8, f32[64,128]{1,0:T(8,128)} %bitcast.9, f32[64,128]{1,0:T(8,128)} %bitcast.10, f32[64,128]{1,0:T(8,128)} %bitcast.11, f32[64,128]{1,0:T(8,128)} %bitcast.12, ...), custom_call_target="tpu_custom_call" | custom-call | tf_op jit(solution)/shard_map/pdhg/pallas_call | solution.py:366
  111.0 1.4 %fusion = (f32[1,64,128]{2,1,0:T(8,128)}, f32[1,64,128]{2,1,0:T(8,128)}) fusion(f32[2,64,128]{2,1,0:T(8,128)} %pdhg.1), kind=kLoop, calls=%fused_computation | loop fusion | bytes 131072 | tf_op jit(solution)/shard_map/slice | solution.py:409

commit v4 on v3

--- a/solution.py
+++ b/solution.py
@@ -21,6 +21,8 @@
 CHUNK = 64
 CUTS = 2
 ROWS = CHUNK // CUTS
+RING_CUTS = 4
+RING_ROWS = CHUNK // RING_CUTS
 PARTS = BS // CHUNK
 
 dual_step = 0.3
@@ -106,6 +108,9 @@
     def arrived(ref, recv_sem):
         waiter(ref, recv_sem, recv_sem).wait_recv()
 
+    def ring_rows(h):
+        return pl.ds(h * RING_ROWS, RING_ROWS)
+
     def rows_of(h):
         return pl.ds(h * ROWS, ROWS)
 
@@ -149,7 +154,7 @@
             total = prod[place[r * CB_DEV]]
             for c in range(1, CB_DEV):
                 total += prod[place[r * CB_DEV + c]]
-            ys[it, r * PARTS : (r + 1) * PARTS] = total
+            ys[it, r * PARTS : (r + 1) * PARTS] = total.reshape(PARTS, RING_CUTS, RING_ROWS, BATCH)
 
     def adjoint_sums(it):
         for cb in range(CB_DEV):
@@ -212,8 +217,8 @@
     def ring_split(it, h, far):
         at = wrap(z - far, NZ)
         high, low = split(dg[it, h, at])
-        ds[at, rows_of(h), :BATCH] = high
-        ds[at, rows_of(h), BATCH:] = low
+        ds[at, ring_rows(h), :BATCH] = high
+        ds[at, ring_rows(h), BATCH:] = low
 
     def ring_arrived(it, h, far):
         arrived(dg.at[it, h, 0], dg_recv.at[it, h, far % NZ])
@@ -316,18 +321,18 @@
             gather_plane_last(it, h)
         products(a_hi, a_lo, [cols_ref[0, s] for s in range(SLOTS)], xs)
         image_sums(it)
-        for h in range(CUTS):
+        for h in range(RING_CUTS):
             ring_send(it, h)
-        for h in range(CUTS):
+        for h in range(RING_CUTS):
             ring_relay(it, h)
-        for h in range(CUTS):
+        for h in range(RING_CUTS):
             image = ring_sum(it, h)
-            dual = jnp.maximum(vecs[DUAL, rows_of(h)] + dual_step * (vecs[BOUND, rows_of(h)] - image), 0.0)
-            vecs[DUAL, rows_of(h)] = dual
+            dual = jnp.maximum(vecs[DUAL, ring_rows(h)] + dual_step * (vecs[BOUND, ring_rows(h)] - image), 0.0)
+            vecs[DUAL, ring_rows(h)] = dual
             gather_ring_start(it, h, dual)
-        for h in range(CUTS):
+        for h in range(RING_CUTS):
             gather_ring_relay(it, h)
-        for h in range(CUTS):
+        for h in range(RING_CUTS):
             gather_ring_finish(it, h)
         products(at_hi, at_lo, [rows_ref[0, s] for s in range(SLOTS)], ds)
         adjoint_sums(it)
@@ -350,11 +355,11 @@
                 result[1, rows_of(h), :] = vecs[DUAL, rows_of(h)]
     for it in range(ITERS):
         for h in range(CUTS):
-            direct = dg.at[it, h, pl.ds(0, NZ - 1)]
-            for sem in (xg_send, rz_send, dg_send, rx_send):
-                waiter(direct, sem.at[it, h], sem.at[it, h]).wait_send()
-            for sem in (xc_send, zc_send):
-                waiter(zc.at[it, h], sem.at[it, h], sem.at[it, h]).wait_send()
+            for ref, sem in ((rx, xg_send), (rx, rx_send), (zc, xc_send), (zc, zc_send)):
+                waiter(ref.at[it, h], sem.at[it, h], sem.at[it, h]).wait_send()
+        for h in range(RING_CUTS):
+            for sem in (rz_send, dg_send):
+                waiter(dg.at[it, h, pl.ds(0, NZ - 1)], sem.at[it, h], sem.at[it, h]).wait_send()
 
 
 def on_device(
@@ -382,9 +387,9 @@
             pltpu.VMEM((ITERS, CUTS, 2, NX, NY, ROWS, BATCH), F32),
             pltpu.VMEM((2 * NX * NY, CHUNK, 2 * BATCH), BF16),
             pltpu.VMEM((SLOTS + 1, PARTS, CUTS, ROWS, BATCH), F32),
-            pltpu.VMEM((ITERS, NZ, CUTS, ROWS, BATCH), F32),
-            pltpu.VMEM((ITERS, CUTS, 2, 8, ROWS, BATCH), F32),
-            pltpu.VMEM((ITERS, CUTS, NZ, ROWS, BATCH), F32),
+            pltpu.VMEM((ITERS, NZ, RING_CUTS, RING_ROWS, BATCH), F32),
+            pltpu.VMEM((ITERS, RING_CUTS, 2, 8, RING_ROWS, BATCH), F32),
+            pltpu.VMEM((ITERS, RING_CUTS, NZ, RING_ROWS, BATCH), F32),
             pltpu.VMEM((NZ, CHUNK, 2 * BATCH), BF16),
             pltpu.VMEM((ITERS, CUTS, 2, NX, NY, ROWS, BATCH), F32),
             pltpu.VMEM((ITERS, CUTS, NX, NY, ROWS, BATCH), F32),
@@ -392,8 +397,8 @@
             dma, dma((3,)), dma((7,)),
             dma((ITERS, CUTS)), dma((ITERS, CUTS, NX)),
             dma((ITERS, CUTS)), dma((ITERS, CUTS, NX)),
-            dma((ITERS, CUTS)), dma((ITERS, CUTS, 2, 3)),
-            dma((ITERS, CUTS)), dma((ITERS, CUTS, NZ)),
+            dma((ITERS, RING_CUTS)), dma((ITERS, RING_CUTS, 2, 3)),
+            dma((ITERS, RING_CUTS)), dma((ITERS, RING_CUTS, NZ)),
             dma((ITERS, CUTS)), dma((ITERS, CUTS, NX)),
             dma((ITERS, CUTS)), dma((ITERS, CUTS)),
         ],

time: 113 us -> 112 us (level)
  no operation moved by 1% of the time
where the time goes in v4:
time: 112 us
  Pallas kernels  110 us (98%)
  local copies, waits for them, and re-layouts  1.4 us (1%)
  between operations  1.29 us (1%)
    pallas_call x1, Pallas kernels, on_device(): pl.pallas_call(kernel, out_shape=jax.ShapeDtypeStruct((2, CHUNK, BATCH),...  110 us

profile of v4, /device:TPU:1, one launch (start us, length us, event | category | flops | bytes accessed | tf_op | source)
XLA Modules:
  0.0 112.2 jit_solution(11317040963250587192)
XLA Ops:
  1.3 109.5 %pdhg.1 = f32[2,64,128]{2,1,0:T(8,128)} custom-call(s32[1,12]{1,0:T(1,128)} %rows_hbm.1, s32[1,12]{1,0:T(1,128)} %cols_hbm.1, s32[1,1]{1,0:T(1,128)S(6)} %copy.13.live_hbm, f32[12,256,256]{2,1,0:T(8,128)} %bitcast.8, f32[64,128]{1,0:T(8,128)} %bitcast.9, f32[64,128]{1,0:T(8,128)} %bitcast.10, f32[64,128]{1,0:T(8,128)} %bitcast.11, f32[64,128]{1,0:T(8,128)} %bitcast.12, ...), custom_call_target="tpu_custom_call" | custom-call | tf_op jit(solution)/shard_map/pdhg/pallas_call | solution.py:371
  110.8 1.4 %fusion = (f32[1,64,128]{2,1,0:T(8,128)}, f32[1,64,128]{2,1,0:T(8,128)}) fusion(f32[2,64,128]{2,1,0:T(8,128)} %pdhg.1), kind=kLoop, calls=%fused_computation | loop fusion | bytes 131072 | tf_op jit(solution)/shard_map/slice | solution.py:414
